TPU v7x, 128 devices: a whole 4x4x4 slice. The times are simulated.
128 devices in a mesh: clip: 4 (over x), rows: 32 (over y, z, core).
Axes of the slice: x: 4, y: 4, z: 4, core: 2. Of those that a mesh axis runs over, the one named last changes fastest.
Arguments:
- latents: bfloat16 [32, 320, 128, 128], P('clip', None, 'rows'), may hold values from -48 to 48
- time_embed: bfloat16 [32, 1280], P('clip'), may hold values from -6 to 6
- time_weight: bfloat16 [1280, 320], replicated, may hold values from -0.15625 to 0.15625
- gain_one: float32 [320], replicated, may hold values from 0.25 to 1.75
- shift_one: float32 [320], replicated, may hold values from -4 to 4
- conv_one: bfloat16 [3, 3, 320, 320], replicated, may hold values from -0.109375 to 0.109375
- bias_one: float32 [320], replicated, may hold values from -4 to 4
- gain_two: float32 [320], replicated, may hold values from 0.25 to 1.75
- shift_two: float32 [320], replicated, may hold values from -4 to 4
- conv_two: bfloat16 [3, 3, 320, 320], replicated, may hold values from -0.109375 to 0.109375
- bias_two: float32 [320], replicated, may hold values from -4 to 4
- send_order: int32 [4, 8192], P('clip', 'rows'), may hold values from 0 to 255, as said below
Outputs:
- block_out: bfloat16 [32, 320, 128, 128], P('clip', None, 'rows')
- student_tokens: bfloat16 [4, 320, 8192], P('clip', None, 'rows')
Inputs may be any that keep to these rules, and one draw needn't show every extreme that they name: `send_order`: each block of 256 consecutive entries of a row (one band of a clip) is a permutation of 0 to 255.
All inputs are finite; a program needn't handle non-finite values.
Results may differ from a plain program's by a relative error of at most 0.0039.
Values may be sent and summed in bfloat16 or wider, within the bound.
A program may use at most 192 MiB of HBM per device.

v0:
```python
import jax
import jax.numpy as jnp
from jax import lax
from jax.sharding import PartitionSpec as P

GROUPS = 32


def with_halo(array, sides, width):
    for axis, dim in sides:
        count, length = (lax.axis_size(axis), array.shape[dim])
        up = [(i, (i + 1) % count) for i in range(count - 1)]
        down = [(j, i) for i, j in up]
        last = lax.slice_in_dim(array, length - width, length, axis=dim)
        leading = lax.slice_in_dim(array, 0, width, axis=dim)
        before = lax.ppermute(last, axis, up)
        after = lax.ppermute(leading, axis, down)
        array = jnp.concatenate([before, array, after], axis=dim)
    return array


def group_moments(values, entries):
    frames, channels, height, width = values.shape
    grouped = values.reshape(frames, GROUPS, channels // GROUPS, height, width)
    totals = lax.psum(jnp.sum(grouped, axis=(2, 3, 4)), "rows")
    group_mean = totals / entries
    deviation = grouped - group_mean[:, :, None, None, None]
    squares = lax.psum(jnp.sum(deviation * deviation, axis=(2, 3, 4)), "rows")
    group_var = squares / entries
    return (group_mean, group_var)


def activate(values, group_mean, group_var, gain, shift):
    frames, channels, height, width = values.shape
    grouped = values.reshape(frames, GROUPS, channels // GROUPS, height, width)
    scaled = (grouped - group_mean[:, :, None, None, None]) * lax.rsqrt(group_var + 1e-05)[
        :, :, None, None, None
    ]
    normed = (
        scaled.reshape(frames, channels, height, width) * gain[None, :, None, None]
        + shift[None, :, None, None]
    )
    return jax.nn.silu(normed)


def convolve(padded, weight):
    out_rows = padded.shape[2] - 2
    columns = padded.shape[3]
    framed = jnp.pad(padded, ((0, 0), (0, 0), (0, 0), (1, 1)))
    total = None
    for row_tap in range(3):
        for col_tap in range(3):
            window = framed[:, :, row_tap : row_tap + out_rows, col_tap : col_tap + columns]
            term = jnp.einsum(
                "oc,fchw->fohw",
                weight[row_tap, col_tap],
                window,
                preferred_element_type=jnp.float32,
            )
            total = term if total is None else total + term
    return total


def with_rims(active):
    return with_halo(active, (("rows", 2),), 1)


def body(
    latents,
    time_embed,
    time_weight,
    gain_one,
    shift_one,
    conv_one,
    bias_one,
    gain_two,
    shift_two,
    conv_two,
    bias_two,
    send_order,
):
    frames, channels, band_rows, columns = latents.shape
    height = band_rows * lax.axis_size("rows")
    entries = channels // GROUPS * height * columns
    values = latents.astype(jnp.float32)
    time_act = jax.nn.silu(time_embed.astype(jnp.float32)).astype(jnp.bfloat16)
    time_proj = jnp.dot(time_act, time_weight, preferred_element_type=jnp.float32)
    offset_one = (bias_one[None, :] + time_proj)[:, :, None, None]
    mean_one, var_one = group_moments(values, entries)
    act_one = activate(values, mean_one, var_one, gain_one, shift_one).astype(jnp.bfloat16)
    hidden_one = (convolve(with_rims(act_one), conv_one) + offset_one).astype(jnp.bfloat16)
    hidden_float = hidden_one.astype(jnp.float32)
    mean_two, var_two = group_moments(hidden_float, entries)
    act_two = activate(hidden_float, mean_two, var_two, gain_two, shift_two).astype(jnp.bfloat16)
    branch = convolve(with_rims(act_two), conv_two)
    result = values + bias_two[None, :, None, None] + branch
    block_out = result.astype(jnp.bfloat16)
    pooled = (
        result.reshape(frames, channels, band_rows // 4, 4, columns // 4, 4)
        .mean(axis=(3, 5))
        .astype(jnp.bfloat16)
    )
    local_cols = jnp.transpose(pooled, (1, 0, 2, 3)).reshape(channels, -1)
    chosen = jnp.take(local_cols, send_order[0], axis=1)
    moved = lax.all_to_all(chosen, "rows", split_axis=1, concat_axis=1, tiled=True)
    return (block_out, moved[None])


def solution(mesh):
    return jax.shard_map(
        body,
        mesh=mesh,
        in_specs=(
            P("clip", None, "rows", None),
            P("clip", None),
            P(),
            P(),
            P(),
            P(),
            P(),
            P(),
            P(),
            P(),
            P(),
            P("clip", "rows"),
        ),
        out_specs=(P("clip", None, "rows", None), P("clip", None, "rows")),
        check_vma=False,
    )
```

profile of v0, /device:TPU:1, one launch (start us, length us, event | category | flops | bytes accessed | tf_op | source)
XLA Modules:
  0.0 439.9 jit_solution(9615785725024850006)
XLA Ops:
  0.7 2.4 convert_reduce_fusion
  3.1 0.8 reduce_sum.60
  3.9 1.0 reduce_sum.61
  4.9 65.1 %psum.28 = f32[8,32]{1,0:T(8,128)S(1)} all-reduce(f32[8,32]{1,0:T(8,128)S(1)} %reduce_sum.61), channel_id=1, replica_groups=mesh['clip'=4,'rows'=32] {'rows'}, use_global_device_ids=true, to_apply=%region_2.3 | all-reduce | flops 256 | bytes 2048 | tf_op jit(solution)/shard_map/psum | solution.py:25
  70.7 1.0 sub.37
  71.8 2.6 fusion.8
  75.1 1.0 reduce_sum.67
  76.2 67.1 %psum.29 = f32[8,32]{1,0:T(8,128)S(1)} all-reduce(f32[8,32]{1,0:T(8,128)S(1)} %reduce_sum.67), channel_id=1, replica_groups=mesh['clip'=4,'rows'=32] {'rows'}, use_global_device_ids=true, to_apply=%region_5.6 | all-reduce | flops 256 | bytes 2048 | tf_op jit(solution)/shard_map/psum | solution.py:28
  144.0 1.0 mul.63
  145.0 2.6 fusion.16
  147.7 1.9 collective-permute-start
  149.7 2.4 collective-permute-start.1
  152.5 3.9 fusion.79
  156.4 0.8 collective-permute-done
  157.2 4.4 collective-permute-done.1
  161.6 5.4 %fusion.5 = bf16[8,320,6,130]{3,1,2,0:T(8,128)(2,1)S(1)} fusion(bf16[8,320,1,128]{3,1,2,0:T(8,128)(2,1)S(1)} %collective-permute-done.1, bf16[8,320,4,128]{3,1,2,0:T(8,128)(2,1)S(1)} %fusion.16, bf16[8,320,1,128]{3,1,2,0:T(8,128)(2,1)S(1)} %collective-permute-done), kind=kLoop, calls=%fused_computation.10 | loop fusion | flops 23961600 | bytes 7925760 | tf_op jit(solution)/shard_map/concatenate | solution.py:18
  167.0 4.2 fusion.49
  171.3 4.0 fusion.51
  175.2 3.8 fusion.53
  179.0 4.0 fusion.55
  183.0 3.8 fusion.59
  186.8 3.8 fusion.47
  190.6 3.8 fusion.57
  194.5 16.4 %bitcast_reduce_fusion = (f32[8,320]{1,0:T(8,128)S(1)}, bf16[8,4,128,320]{2,3,1,0:T(8,128)(2,1)S(1)}) fusion(f32[8,320]{1,0:T(8,128)S(1)} %convolution_add_fusion, bf16[8,320,6,130]{3,1,2,0:T(8,128)(2,1)} %copy-done.2, bf16[3,3,320,320]{3,2,1,0:T(8,128)(2,1)} %param.17, f32[8,4,128,320]{2,3,1,0:T(8,128)} %fusion.47, f32[8,4,128,320]{2,3,1,0:T(8,128)} %fusion.49, ...), kind=kOutput, calls=%fused_computation.27 | convolution fusion | flops 854586880 | bytes 47452160 | tf_op jit(solution)/shard_map/oc,fchw->fohw/dot_general | solution.py:54
  211.2 68.5 %psum.30 = f32[8,32]{1,0:T(8,128)S(1)} all-reduce(f32[8,32]{1,0:T(8,128)S(1)} %reduce_sum.70), channel_id=1, replica_groups=mesh['clip'=4,'rows'=32] {'rows'}, use_global_device_ids=true, to_apply=%region_8.9 | all-reduce | flops 256 | bytes 2048 | tf_op jit(solution)/shard_map/psum | solution.py:25
  279.9 1.4 fusion.20
  281.6 68.3 %psum.31 = f32[8,32]{1,0:T(8,128)S(1)} all-reduce(f32[8,32]{1,0:T(8,128)S(1)} %reduce_sum.91), channel_id=1, replica_groups=mesh['clip'=4,'rows'=32] {'rows'}, use_global_device_ids=true, to_apply=%region_11.12 | all-reduce | flops 256 | bytes 2048 | tf_op jit(solution)/shard_map/psum | solution.py:28
  350.1 3.9 fusion.28
  354.0 1.1 fusion.116
  355.1 1.9 collective-permute-start.2
  357.1 2.4 collective-permute-start.3
  360.8 4.8 %fusion.69 = f32[8,4,128,320]{2,3,1,0:T(8,128)} fusion(bf16[8,320,4,128]{3,1,2,0:T(8,128)(2,1)S(1)} %fusion.28, bf16[3,3,320,320]{3,2,1,0:T(8,128)(2,1)} %param.21), kind=kOutput, calls=%fused_computation.83 | convolution fusion | flops 838860800 | bytes 8110080 | tf_op jit(solution)/shard_map/oc,fchw->fohw/dot_general | solution.py:54
  365.6 3.7 collective-permute-done.3
  369.3 6.0 %select_maximum_fusion = bf16[8,320,6,130]{3,1,2,0:T(8,128)(2,1)S(1)} fusion(bf16[8,320,1,128]{3,1,2,0:T(8,128)(2,1)} %collective-permute-done.3, bf16[8,320,4,128]{3,1,2,0:T(8,128)(2,1)S(1)} %fusion.28, bf16[8,320,1,128]{3,1,2,0:T(8,128)(2,1)S(1)} %collective-permute-done.2), kind=kLoop, calls=%fused_computation.4 | loop fusion | flops 23961600 | bytes 7925760 | tf_op jit(solution)/shard_map/concatenate | solution.py:18
  375.3 4.5 %fusion.33 = f32[8,4,128,320]{2,3,1,0:T(8,128)} fusion(bf16[8,320,6,130]{3,1,2,0:T(8,128)(2,1)S(1)} %select_maximum_fusion, bf16[3,3,320,320]{3,2,1,0:T(8,128)(2,1)S(1)} %copy-done.7), kind=kOutput, calls=%fused_computation.45 | convolution fusion | flops 838860800 | bytes 8110080 | tf_op jit(solution)/shard_map/oc,fchw->fohw/dot_general | solution.py:54
  379.8 4.0 fusion.35
  383.8 3.8 fusion.37
  387.6 4.0 fusion.39
  391.6 3.8 fusion.43
  395.4 3.8 fusion.41
  399.2 4.9 %fusion.31 = f32[8,4,128,320]{2,3,1,0:T(8,128)} fusion(bf16[8,320,1,128]{3,1,2,0:T(8,128)(2,1)} %collective-permute-done.3, bf16[8,320,4,128]{3,1,2,0:T(8,128)(2,1)S(1)} %fusion.28, bf16[3,3,320,320]{3,2,1,0:T(8,128)(2,1)S(1)} %copy-done.7), kind=kOutput, calls=%fused_computation.43 | convolution fusion | flops 844103680 | bytes 8765440 | tf_op jit(solution)/shard_map/oc,fchw->fohw/dot_general | solution.py:54
  404.1 19.8 %fusion.115 = (f32[8,320,128]{2,1,0:T(8,128)}, bf16[8,320,4,128]{3,1,2,0:T(8,128)(2,1)}) fusion(bf16[8,320,6,130]{3,1,2,0:T(8,128)(2,1)} %copy-done.3, bf16[3,3,320,320]{3,2,1,0:T(8,128)(2,1)} %param.21, f32[8,4,128,320]{2,3,1,0:T(8,128)} %fusion.31, f32[8,4,128,320]{2,3,1,0:T(8,128)} %fusion.33, f32[8,4,128,320]{2,3,1,0:T(8,128)} %fusion.35, ...), kind=kOutput, calls=%fused_computation.139 | convolution fusion | flops 855572480 | bytes 51365120 | tf_op jit(solution)/shard_map/oc,fchw->fohw/dot_general | solution.py:54
  423.9 2.0 copy.21
  426.1 1.2 gather_fusion
  428.1 3.6 all-to-all-start
  431.7 5.3 %copy.23 = bf16[8,320,4,128]{3,2,1,0:T(4,128)(2,1)} copy(bf16[8,320,4,128]{3,1,2,0:T(8,128)(2,1)} %get-tuple-element.9) | data formatting | bytes 5242880
  437.0 1.9 all-to-all-done
  438.9 0.8 copy.24
  (60 shorter events, 6.0 us)
Async XLA Ops:
  0.6 151.5 %copy-start = (bf16[1280,320]{0,1:T(8,128)(2,1)S(1)}, bf16[1280,320]{0,1:T(8,128)(2,1)}, u32[]{:S(2)}) copy-start(bf16[1280,320]{0,1:T(8,128)(2,1)} %param.14) | copy-start | bytes 2457604
  0.6 144.4 %copy-start.4 = (bf16[8,320,4,128]{3,2,1,0:T(4,128)(2,1)S(1)}, bf16[8,320,4,128]{3,2,1,0:T(4,128)(2,1)}, u32[]{:S(2)}) copy-start(bf16[8,320,4,128]{3,2,1,0:T(4,128)(2,1)} %param.12) | copy-start | bytes 7864324
  0.7 144.4 %copy-start.11 = (f32[320]{0:T(512)S(1)}, f32[320]{0:T(512)}, u32[]{:S(2)}) copy-start(f32[320]{0:T(512)} %param.15) | copy-start | bytes 3844
  0.7 144.4 %copy-start.10 = (f32[320]{0:T(512)S(1)}, f32[320]{0:T(512)}, u32[]{:S(2)}) copy-start(f32[320]{0:T(512)} %param.16) | copy-start | bytes 3844
  71.7 80.4 %copy-start.8 = (bf16[8,1280]{1,0:T(8,128)(2,1)S(1)}, bf16[8,1280]{1,0:T(8,128)(2,1)}, u32[]{:S(2)}) copy-start(bf16[8,1280]{1,0:T(8,128)(2,1)} %param.13) | copy-start | bytes 61444
  71.8 80.4 %copy-start.12 = (f32[320]{0:T(512)S(1)}, f32[320]{0:T(512)}, u32[]{:S(2)}) copy-start(f32[320]{0:T(512)} %param.18) | copy-start | bytes 3844
  74.3 78.1 %copy-start.9 = (s32[1,256]{1,0:T(1,128)S(1)}, s32[1,256]{1,0:T(1,128)}, u32[]{:S(2)}) copy-start(s32[1,256]{1,0:T(1,128)} %param.23) | copy-start | bytes 3076
  145.0 7.4 %copy-start.6 = (bf16[3,3,320,320]{3,2,1,0:T(8,128)(2,1)S(1)}, bf16[3,3,320,320]{3,2,1,0:T(8,128)(2,1)}, u32[]{:S(2)}) copy-start(bf16[3,3,320,320]{3,2,1,0:T(8,128)(2,1)} %param.17) | copy-start | bytes 5529604
  147.7 9.4 %collective-permute-start = (bf16[8,320,1,128]{3,1,2,0:T(8,128)(2,1)S(1)}, bf16[8,320,1,128]{3,1,2,0:T(8,128)(2,1)S(1)}, u32[]{:S(2)}, u32[]{:S(2)}) collective-permute-start(bf16[8,320,1,128]{3,1,2,0:T(8,128)(2,1)S(1)} %get-tuple-element.12), channel_id=1, source_target_pairs={{0,1},{1,2},{2,3},{3,4},{4,5},{5,6},{6,7},{7,8},{8,9},{9,10},{10,1... | collective-permute-start | bytes 1966088 | tf_op jit(solution)/shard_map/ppermute | solution.py:16
  149.7 11.9 %collective-permute-start.1 = (bf16[8,320,1,128]{3,1,2,0:T(8,128)(2,1)S(1)}, bf16[8,320,1,128]{3,1,2,0:T(8,128)(2,1)S(1)}, u32[]{:S(2)}, u32[]{:S(2)}) collective-permute-start(bf16[8,320,1,128]{3,1,2,0:T(8,128)(2,1)S(1)} %get-tuple-element.13), channel_id=1, source_target_pairs={{1,0},{2,1},{3,2},{4,3},{5,4},{6,5},{7,6},{8,7},{9,8},{10,9},{11,1... | collective-permute-start | bytes 1966088 | tf_op jit(solution)/shard_map/ppermute | solution.py:17
  167.0 16.0 %copy-start.2 = (bf16[8,320,6,130]{3,1,2,0:T(8,128)(2,1)}, bf16[8,320,6,130]{3,1,2,0:T(8,128)(2,1)S(1)}, u32[]{:S(2)}) copy-start(bf16[8,320,6,130]{3,1,2,0:T(8,128)(2,1)S(1)} %fusion.5) | copy-start | bytes 11980804
  194.5 155.6 %copy-start.13 = (f32[320]{0:T(512)S(1)}, f32[320]{0:T(512)}, u32[]{:S(2)}) copy-start(f32[320]{0:T(512)} %param.20) | copy-start | bytes 3844
  194.5 155.6 %copy-start.14 = (f32[320]{0:T(512)S(1)}, f32[320]{0:T(512)}, u32[]{:S(2)}) copy-start(f32[320]{0:T(512)} %param.19) | copy-start | bytes 3844
  210.9 139.0 %copy-start.5 = (bf16[8,4,128,320]{2,3,1,0:T(8,128)(2,1)}, bf16[8,4,128,320]{2,3,1,0:T(8,128)(2,1)S(1)}, u32[]{:S(2)}) copy-start(bf16[8,4,128,320]{2,3,1,0:T(8,128)(2,1)S(1)} %get-tuple-element.15) | copy-start | bytes 7864324
  355.1 10.4 %collective-permute-start.2 = (bf16[8,320,1,128]{3,1,2,0:T(8,128)(2,1)}, bf16[8,320,1,128]{3,1,2,0:T(8,128)(2,1)S(1)}, u32[]{:S(2)}, u32[]{:S(2)}) collective-permute-start(bf16[8,320,1,128]{3,1,2,0:T(8,128)(2,1)} %get-tuple-element.10), channel_id=1, source_target_pairs={{0,1},{1,2},{2,3},{3,4},{4,5},{5,6},{6,7},{7,8},{8,9},{9,10},{10,1... | collective-permute-start | bytes 1966088 | tf_op jit(solution)/shard_map/ppermute | solution.py:16
  357.1 12.2 %collective-permute-start.3 = (bf16[8,320,1,128]{3,1,2,0:T(8,128)(2,1)}, bf16[8,320,1,128]{3,1,2,0:T(8,128)(2,1)}, u32[]{:S(2)}, u32[]{:S(2)}) collective-permute-start(bf16[8,320,1,128]{3,1,2,0:T(8,128)(2,1)} %get-tuple-element.11), channel_id=1, source_target_pairs={{1,0},{2,1},{3,2},{4,3},{5,4},{6,5},{7,6},{8,7},{9,8},{10,9},{11,1... | collective-permute-start | bytes 1966088 | tf_op jit(solution)/shard_map/ppermute | solution.py:17
  365.6 9.7 %copy-start.7 = (bf16[3,3,320,320]{3,2,1,0:T(8,128)(2,1)S(1)}, bf16[3,3,320,320]{3,2,1,0:T(8,128)(2,1)}, u32[]{:S(2)}) copy-start(bf16[3,3,320,320]{3,2,1,0:T(8,128)(2,1)} %param.21) | copy-start | bytes 5529604
  375.3 16.2 %copy-start.3 = (bf16[8,320,6,130]{3,1,2,0:T(8,128)(2,1)}, bf16[8,320,6,130]{3,1,2,0:T(8,128)(2,1)S(1)}, u32[]{:S(2)}) copy-start(bf16[8,320,6,130]{3,1,2,0:T(8,128)(2,1)S(1)} %select_maximum_fusion) | copy-start | bytes 11980804
  399.2 4.9 %copy-start.15 = (f32[320]{0:T(512)S(1)}, f32[320]{0:T(512)}, u32[]{:S(2)}) copy-start(f32[320]{0:T(512)} %param.22) | copy-start | bytes 3844
  423.9 15.8 %copy-start.1 = (bf16[1280,320]{0,1:T(8,128)(2,1)S(1)}, bf16[1280,320]{0,1:T(8,128)(2,1)}, u32[]{:S(2)}) copy-start(bf16[1280,320]{0,1:T(8,128)(2,1)} %param.14) | copy-start | bytes 2457604
  428.1 10.8 %all-to-all-start = ((bf16[320,32,8]{0,2,1:T(8,128)(2,1)}), bf16[320,32,8]{0,2,1:T(8,128)(2,1)S(1)}, u32[]{:S(2)}, u32[]{:S(2)}) async-start(bf16[320,32,8]{0,2,1:T(8,128)(2,1)} %bitcast_select_fusion), calls=%async_computation | async-start | bytes 393216 | tf_op jit(solution)/shard_map/all_to_all | solution.py:105
where the time goes:
time: 444 us; the launch traced here: 440 us
  blocking collectives  269 us (61%)
  matrix products  101 us (23%)
  other arithmetic  28.2 us (6%)
  local copies, waits for them, and re-layouts  17 us (4%)
  starting transfers between devices  12.4 us (3%)
  waiting for transfers between devices  10.8 us (2%)
    psum x2, blocking collectives, group_moments(): squares = lax.psum(jnp.sum(deviation * deviation, axis=(2, 3, 4)), 'rows')  135 us
    psum x2, blocking collectives, group_moments(): totals = lax.psum(jnp.sum(grouped, axis=(2, 3, 4)), 'rows')  134 us
    dot_general x18, matrix products, convolve(): jnp.einsum('oc,fchw->fohw', weight[row_tap, col_tap], window, preferred_e...  101 us
    concatenate x2, other arithmetic, with_halo(): array = jnp.concatenate([before, array, after], axis=dim)  11.5 us
  transfers between devices with their start and end apart: 5, of which 4 were waited for; matrix products, arithmetic and copies ran while one was open for 4% of the time, Pallas kernels for 0%

commit v1 on v0

v1 whole, which is shorter than its diff:
```python
import functools

import jax
import jax.numpy as jnp
from jax import lax
from jax.experimental import pallas as pl
from jax.experimental.pallas import tpu as pltpu
from jax.sharding import PartitionSpec as P

F32 = jnp.float32
BF16 = jnp.bfloat16
C = 320
CP = 384
GROUPS = 32
PER = C // GROUPS
W = 128
R = 4
FR = 8
ND = 32
NG = 2
FG = FR // NG
EXACT = lax.Precision.HIGHEST
MESH = pl.DeviceIdType.MESH


def dot(a, b, precision=None):
    return jnp.dot(a, b, preferred_element_type=F32, precision=precision)


def to_row(x):
    return jnp.sum(jnp.transpose(x), axis=0, keepdims=True)


def to_cols(row):
    return jnp.transpose(jnp.broadcast_to(row, (W, C)))


def group_lanes(first):
    chan = lax.broadcasted_iota(jnp.int32, (C, W), 0) // PER
    lane = lax.broadcasted_iota(jnp.int32, (C, W), 1)
    return jnp.where(chan + first == lane, 1.0, 0.0).astype(F32)


def group_rows():
    chan = lax.broadcasted_iota(jnp.int32, (W, C), 1) // PER
    lane = lax.broadcasted_iota(jnp.int32, (W, C), 0)
    return jnp.where(chan == lane, 1.0, 0.0).astype(F32)


def place_weights(raw, packed):
    for b in range(3):
        rows = slice(b * C, (b + 1) * C)
        for a in range(3):
            packed[rows, a * 256 : (a + 1) * 256] = raw[a * 3 + b, :, 0:256]
        packed[rows, 768:960] = jnp.concatenate([raw[a * 3 + b, :, 256:C] for a in range(3)], axis=1)


def conv_half(act, packed, half):
    lane = lax.broadcasted_iota(jnp.int32, (C, W), 1)
    at = [slice((half * 2 + a) * W, (half * 2 + a) * W + 2 * W) for a in range(3)]
    rhs = jnp.concatenate(
        [act[0:256, at[a]] for a in range(3)] + [act[256:C, at[a]] for a in range(3)], axis=0
    )
    y = [dot(packed[b * C : (b + 1) * C, :], rhs) for b in range(3)]
    rows = []
    for r in range(2):
        s = slice(r * W, (r + 1) * W)
        left = jnp.where(lane == 0, 0.0, pltpu.roll(y[0][:, s], 1, 1))
        right = jnp.where(lane == W - 1, 0.0, pltpu.roll(y[2][:, s], W - 1, 1))
        rows.append(y[1][:, s] + left + right)
    return rows


def main_kernel(
    lat, temb, tw, gain1, shift1, w1, bias1, gain2, shift2, w2, bias2, order,
    res, tok,
    lraw, wide, x6, h6, act, raw1, raw2, pk1, pk2, resbuf, psum,
    rowsum, pivot, sq, gath, msg, coef, offs, tsend, trecv,
    in_sem, w_sem, out_sem, halo_send, halo_recv, ag_send, ag_recv, tok_send, tok_recv,
):
    clip, me = lax.axis_index("clip"), lax.axis_index("rows")
    up, down = lax.rem(me + ND - 1, ND), lax.rem(me + 1, ND)
    n_local = float(PER * R * W)

    def partner(k):
        return lax.rem(me + k, ND)

    barrier = pltpu.get_barrier_semaphore()

    def greet(k, carry):
        pl.semaphore_signal(barrier, inc=1, device_id=(clip, partner(k)), device_id_type=MESH)
        return carry

    lax.fori_loop(1, ND, greet, 0)

    fetch = [pltpu.make_async_copy(lat.at[f], lraw.at[f], in_sem.at[f]) for f in range(FR)]
    for copy in fetch:
        copy.start()
    wfetch = [
        pltpu.make_async_copy(w1, raw1, w_sem.at[0]),
        pltpu.make_async_copy(w2, raw2, w_sem.at[1]),
    ]
    for copy in wfetch:
        copy.start()

    def halo_copies(stage, g):
        buf = (x6, h6)[stage]
        frames = pl.ds(g * FG, FG)
        return [
            pltpu.make_async_remote_copy(
                src_ref=buf.at[src, frames], dst_ref=buf.at[dst, frames],
                send_sem=halo_send.at[stage, g, i], recv_sem=halo_recv.at[stage, g, i],
                device_id=(clip, to), device_id_type=MESH,
            )
            for i, (src, dst, to) in enumerate(((1, 5, up), (4, 0, down)))
        ]

    def ag_copy(slot, k):
        return pltpu.make_async_remote_copy(
            src_ref=msg.at[slot], dst_ref=gath.at[slot, me],
            send_sem=ag_send.at[slot, k], recv_sem=ag_recv.at[slot, k],
            device_id=(clip, partner(k)), device_id_type=MESH,
        )

    def ag_start(slot):
        gath[slot, me] = msg[slot]

        def one(k, carry):
            ag_copy(slot, k).start()
            return carry

        lax.fori_loop(1, ND, one, 0)

    def ag_wait(slot):
        def one(k, carry):
            ag_copy(slot, k).wait()
            return carry

        lax.fori_loop(1, ND, one, 0)

    def stats(slot, stage, g):
        buf = (x6, h6)[stage]
        gl = group_lanes(0)
        mean = dot(rowsum[...], gl, EXACT) / n_local
        pivot[...] = dot(mean, group_rows(), EXACT)

        def one(j, carry):
            middle = to_cols(pivot[pl.ds(j, 1), :])
            total = None
            for r in range(R):
                d = buf[r + 1, g * FG + j].astype(F32) - middle
                total = d * d if total is None else total + d * d
            sq[pl.ds(j, 1), :] = to_row(total)
            return carry

        lax.fori_loop(0, FG, one, 0)
        msg[slot] = mean + dot(sq[...], group_lanes(GROUPS), EXACT)

    def coefs(slot, gain, shift):
        every = gath[slot]
        lane = lax.broadcasted_iota(jnp.int32, (8, W), 1)
        mean = jnp.sum(every, axis=0) * (1.0 / ND)
        away = every - mean[None]
        spread = jnp.sum(away * away, axis=0) * n_local
        inner = pltpu.roll(jnp.sum(every, axis=0), W - GROUPS, 1)
        var = (spread + inner) * (1.0 / (ND * n_local))
        valid = lane < GROUPS
        inv = jnp.where(valid, lax.rsqrt(jnp.where(valid, var, 1.0) + 1e-5), 0.0)
        gr = group_rows()
        scale = dot(inv, gr, EXACT) * gain[...]
        offset = shift[...] - dot(jnp.where(valid, mean, 0.0), gr, EXACT) * scale
        coef[0] = scale * 0.5
        coef[1] = offset * 0.5

    def activate(buf, f, j):
        sc = to_cols(coef[0, pl.ds(j, 1), :])
        sh = to_cols(coef[1, pl.ds(j, 1), :])
        for row in range(R + 2):
            h = buf[row, f].astype(F32) * sc + sh
            a = h * jnp.tanh(h) + h
            if row == 0:
                a = jnp.where(me > 0, a, 0.0)
            if row == R + 1:
                a = jnp.where(me < ND - 1, a, 0.0)
            act[:, row * W : (row + 1) * W] = a.astype(BF16)

    rowsum[...] = jnp.zeros((8, C), F32)
    sq[...] = jnp.zeros((8, C), F32)

    def split(f, carry):
        pltpu.make_async_copy(lat.at[f], lraw.at[f], in_sem.at[f]).wait()
        wide[...] = lraw[f].astype(F32)
        total = None
        for r in range(R):
            x = wide[pl.ds(r, C, stride=R), :]
            x6[r + 1, f] = x.astype(BF16)
            total = x if total is None else total + x
        rowsum[pl.ds(lax.rem(f, FG), 1), :] = to_row(total)
        return carry

    for g in range(NG):
        lax.fori_loop(g * FG, (g + 1) * FG, split, 0)
        if g == 0:
            pl.semaphore_wait(barrier, ND - 1)
        for copy in halo_copies(0, g):
            copy.start()
        stats(g, 0, g)
        ag_start(g)

    embed = temb[...].astype(F32)
    tact = (embed / (1.0 + jnp.exp(-embed))).astype(BF16)
    offs[...] = dot(tact, tw[...]) + bias1[...]
    wfetch[0].wait()
    place_weights(raw1, pk1)
    wfetch[1].wait()
    place_weights(raw2, pk2)

    for g in range(NG):
        ag_wait(g)
        for copy in halo_copies(0, g):
            copy.wait()
        coefs(g, gain1, shift1)

        def first(j, carry):
            f = g * FG + j
            activate(x6, f, j)
            off = to_cols(offs[pl.ds(f, 1), :])
            total = None
            for half in range(2):
                for i, y in enumerate(conv_half(act, pk1, half)):
                    h = (y + off).astype(BF16)
                    h6[half * 2 + i + 1, f] = h
                    h = h.astype(F32)
                    total = h if total is None else total + h
            rowsum[pl.ds(j, 1), :] = to_row(total)
            return carry

        lax.fori_loop(0, FG, first, 0)
        for copy in halo_copies(1, g):
            copy.start()
        stats(NG + g, 1, g)
        ag_start(NG + g)

    tail = to_cols(bias2[...])

    for g in range(NG):
        ag_wait(NG + g)
        for copy in halo_copies(1, g):
            copy.wait()
        coefs(NG + g, gain2, shift2)

        def second(j, carry):
            f = g * FG + j
            activate(h6, f, j)
            total = None
            for half in range(2):
                for i, y in enumerate(conv_half(act, pk2, half)):
                    r = half * 2 + i
                    v = y + (x6[r + 1, f].astype(F32) + tail)
                    resbuf[f, r] = v.astype(BF16)
                    total = v if total is None else total + v
            psum[f] = total
            pltpu.make_async_copy(resbuf.at[f], res.at[f], out_sem.at[f]).start()
            return carry

        lax.fori_loop(0, FG, second, 0)

    lanes = FR * W
    spot = lax.broadcasted_iota(jnp.int32, (lanes, 256), 0) // 4
    col = lax.broadcasted_iota(jnp.int32, (lanes, 256), 1)
    pool = jnp.where(spot == col, 1.0 / 16.0, 0.0).astype(BF16)
    sums = jnp.concatenate([psum[f] for f in range(FR)], axis=1)
    high = sums.astype(BF16)
    rest = sums - high.astype(F32)
    mid = rest.astype(BF16)
    low = (rest - mid.astype(F32)).astype(BF16)
    pooled = (dot(high, pool) + dot(mid, pool) + dot(low, pool)).astype(BF16)
    patch = lax.broadcasted_iota(jnp.int32, (256, 256), 0)
    pick = jnp.where(patch == order[...], 1.0, 0.0).astype(BF16)
    chosen = dot(pooled, pick)
    placed = jnp.transpose(jnp.concatenate([chosen, jnp.zeros((CP - C, 256), F32)], axis=0))
    placed = placed.reshape(ND, 8, CP)
    lower = jnp.concatenate([placed[:, :, 256:CP], jnp.zeros((ND, 8, 128), F32)], axis=2)
    tsend[...] = jnp.concatenate([placed[:, :, 0:256], lower], axis=1).astype(BF16)
    trecv[me] = tsend[me]

    def tok_copy(k):
        return pltpu.make_async_remote_copy(
            src_ref=tsend.at[partner(k)], dst_ref=trecv.at[me],
            send_sem=tok_send.at[k], recv_sem=tok_recv.at[k],
            device_id=(clip, partner(k)), device_id_type=MESH,
        )

    def tok_start(k, carry):
        tok_copy(k).start()
        return carry

    def tok_wait(k, carry):
        tok_copy(k).wait()
        return carry

    lax.fori_loop(1, ND, tok_start, 0)
    lax.fori_loop(1, ND, tok_wait, 0)
    tok[...] = trecv[...]

    def drain(f, carry):
        pltpu.make_async_copy(resbuf.at[f], res.at[f], out_sem.at[f]).wait()
        return carry

    lax.fori_loop(0, FR, drain, 0)


def finish_kernel(res, tok, out, student, wide):
    for r in range(R):
        wide[pl.ds(r, C, stride=R), :] = res[0, r].astype(F32)
    out[0] = wide[...].astype(BF16)

    @pl.when(pl.program_id(0) == 0)
    def _():
        t = tok[...].astype(F32)
        top = jnp.transpose(t[:, 0:8, :].reshape(256, 256))
        low = jnp.transpose(t[:, 8:16, 0:128].reshape(256, 128))
        student[0] = jnp.concatenate([top, low[0 : C - 256]], axis=0).astype(BF16)


def body(lat, temb, tw, gain1, shift1, w1, bias1, gain2, shift2, w2, bias2, order):
    vm = pl.BlockSpec(memory_space=pltpu.VMEM)
    anyspace = pl.BlockSpec(memory_space=pl.ANY)
    dma = pltpu.SemaphoreType.DMA
    row = lambda v: v.reshape(1, C)
    res, tok = pl.pallas_call(
        main_kernel,
        out_shape=(
            jax.ShapeDtypeStruct((FR, R, C, W), BF16),
            jax.ShapeDtypeStruct((ND, 16, 256), BF16),
        ),
        in_specs=[anyspace, vm, vm, vm, vm, anyspace, vm, vm, vm, anyspace, vm, vm],
        out_specs=(anyspace, vm),
        scratch_shapes=[
            pltpu.VMEM((FR, C * R, W), BF16),
            pltpu.VMEM((C * R, W), F32),
            pltpu.VMEM((R + 2, FR, C, W), BF16),
            pltpu.VMEM((R + 2, FR, C, W), BF16),
            pltpu.VMEM((C, (R + 2) * W), BF16),
            pltpu.VMEM((9, C, C), BF16),
            pltpu.VMEM((9, C, C), BF16),
            pltpu.VMEM((3 * C, 3 * C), BF16),
            pltpu.VMEM((3 * C, 3 * C), BF16),
            pltpu.VMEM((FR, R, C, W), BF16),
            pltpu.VMEM((FR, C, W), F32),
            pltpu.VMEM((8, C), F32),
            pltpu.VMEM((8, C), F32),
            pltpu.VMEM((8, C), F32),
            pltpu.VMEM((2 * NG, ND, 8, W), F32),
            pltpu.VMEM((2 * NG, 8, W), F32),
            pltpu.VMEM((2, 8, C), F32),
            pltpu.VMEM((FR, C), F32),
            pltpu.VMEM((ND, 16, 256), BF16),
            pltpu.VMEM((ND, 16, 256), BF16),
            dma((FR,)),
            dma((2,)),
            dma((FR,)),
            dma((2, NG, 2)),
            dma((2, NG, 2)),
            dma((2 * NG, ND)),
            dma((2 * NG, ND)),
            dma((ND,)),
            dma((ND,)),
        ],
        compiler_params=pltpu.CompilerParams(
            collective_id=0, has_side_effects=True, vmem_limit_bytes=56 * 2**20
        ),
        name="block",
    )(
        lat.reshape(FR, C * R, W), temb, tw, row(gain1), row(shift1), w1.reshape(9, C, C), row(bias1),
        row(gain2), row(shift2), w2.reshape(9, C, C), row(bias2), order,
    )
    out, student = pl.pallas_call(
        finish_kernel,
        grid=(FR,),
        out_shape=(
            jax.ShapeDtypeStruct((FR, C * R, W), BF16),
            jax.ShapeDtypeStruct((1, C, 256), BF16),
        ),
        in_specs=[
            pl.BlockSpec((1, R, C, W), lambda f: (f, 0, 0, 0)),
            pl.BlockSpec((ND, 16, 256), lambda f: (0, 0, 0)),
        ],
        out_specs=(
            pl.BlockSpec((1, C * R, W), lambda f: (f, 0, 0)),
            pl.BlockSpec((1, C, 256), lambda f: (0, 0, 0)),
        ),
        scratch_shapes=[pltpu.VMEM((C * R, W), F32)],
        name="finish",
    )(res, tok)
    return out.reshape(FR, C, R, W), student


def solution(mesh):
    return jax.shard_map(
        body,
        mesh=mesh,
        in_specs=(
            P("clip", None, "rows", None),
            P("clip", None),
            P(), P(), P(), P(), P(), P(), P(), P(), P(),
            P("clip", "rows"),
        ),
        out_specs=(P("clip", None, "rows", None), P("clip", None, "rows")),
        check_vma=False,
    )
```

time: 444 us -> 79.9 us (0.18)
  blocking collectives: 269 us -> 0 us
  matrix products: 101 us -> 0 us
  Pallas kernels: 0 us -> 69.2 us
  other arithmetic: 28.2 us -> 0 us
  starting transfers between devices: 12.4 us -> 0 us
  waiting for transfers between devices: 10.8 us -> 0 us
  local copies, waits for them, and re-layouts: 17 us -> 9.61 us
    psum x4 -> x0, blocking collectives: 269 us -> none  [the longest x2 135 us: group_moments(): squares = lax.psum(jnp.sum(deviation * deviation, axis=(2, 3, 4)), 'rows')]
    dot_general x19 -> x0, matrix products: 101 us -> none  [the longest x18 101 us: convolve(): jnp.einsum('oc,fchw->fohw', weight[row_tap, col_tap], window, preferred_e...]
    pallas_call x0 -> x2, Pallas kernels: none -> 69.2 us  [the longest x1 62.7 us: body(): pl.pallas_call(main_kernel, out_shape=(jax.ShapeDtypeStruct((FR, R, C, W)...]
    concatenate x2 -> x0, other arithmetic: 11.5 us -> none  [with_halo(): array = jnp.concatenate([before, array, after], axis=dim)]
    ppermute x4 -> x0, waiting for transfers between devices: 8.9 us -> none  [the longest x2 8.09 us: with_halo(): after = lax.ppermute(leading, axis, down)]
    ppermute x4 -> x0, starting transfers between devices: 8.72 us -> none  [the longest x2 4.89 us: with_halo(): after = lax.ppermute(leading, axis, down)]
    reduce_sum x8 -> x0, other arithmetic: 8.69 us -> none  [the longest x4 5.08 us: group_moments(): squares = lax.psum(jnp.sum(deviation * deviation, axis=(2, 3, 4)), 'rows')]
    reshape x0 -> x6, local copies, waits for them, and re-layouts: none -> 7.41 us  [body(): row = lambda v: v.reshape(1, C)]
  transfers between devices with their start and end apart: 5 -> 0, of which waited for: 4 -> 0; matrix products, arithmetic and copies ran while one was open for 4% -> 0% of each run, Pallas kernels for 0% -> 0%
where the time goes in v1:
time: 79.9 us; the launch traced here: 79.5 us
  Pallas kernels  69.2 us (87%)
  local copies, waits for them, and re-layouts  9.61 us (12%)
    pallas_call x1, Pallas kernels, body(): pl.pallas_call(main_kernel, out_shape=(jax.ShapeDtypeStruct((FR, R, C, W)...  62.7 us
    reshape x6, local copies, waits for them, and re-layouts, body(): row = lambda v: v.reshape(1, C)  7.41 us
    pallas_call x1, Pallas kernels, body(): pl.pallas_call(finish_kernel, grid=(FR,), out_shape=(jax.ShapeDtypeStruct...  6.49 us
    unnamed x1, local copies, waits for them, and re-layouts  2.2 us

profile of v1, /device:TPU:1, one launch (start us, length us, event | category | flops | bytes accessed | tf_op | source)
XLA Modules:
  0.0 79.5 jit_solution(12615366915621976516)
XLA Ops:
  0.6 1.2 %reshape.35.gain1 = f32[1,320]{1,0:T(1,128)} reshape(f32[320]{0:T(512)} %param.15) | data formatting | bytes 2560 | tf_op jit(solution)/shard_map/reshape | solution.py:330
  1.9 1.2 %reshape.36.shift1 = f32[1,320]{1,0:T(1,128)} reshape(f32[320]{0:T(512)} %param.16) | data formatting | bytes 2560 | tf_op jit(solution)/shard_map/reshape | solution.py:330
  3.1 1.3 %reshape.38.bias1 = f32[1,320]{1,0:T(1,128)} reshape(f32[320]{0:T(512)} %param.18) | data formatting | bytes 2560 | tf_op jit(solution)/shard_map/reshape | solution.py:330
  4.4 1.2 %reshape.39.gain2 = f32[1,320]{1,0:T(1,128)} reshape(f32[320]{0:T(512)} %param.19) | data formatting | bytes 2560 | tf_op jit(solution)/shard_map/reshape | solution.py:330
  5.6 1.2 %reshape.40.shift2 = f32[1,320]{1,0:T(1,128)} reshape(f32[320]{0:T(512)} %param.20) | data formatting | bytes 2560 | tf_op jit(solution)/shard_map/reshape | solution.py:330
  6.8 1.2 %reshape.42.bias2 = f32[1,320]{1,0:T(1,128)} reshape(f32[320]{0:T(512)} %param.22) | data formatting | bytes 2560 | tf_op jit(solution)/shard_map/reshape | solution.py:330
  8.0 2.2 %copy.14.tw = bf16[1280,320]{1,0:T(8,128)(2,1)} copy(bf16[1280,320]{0,1:T(8,128)(2,1)} %param.14) | data formatting | bytes 1638400 | tf_op args[2]
  10.2 62.7 %block.1 = (bf16[8,4,320,128]{3,2,1,0:T(8,128)(2,1)}, bf16[32,16,256]{2,1,0:T(8,128)(2,1)}) custom-call(bf16[8,1280,128]{2,1,0:T(8,128)(2,1)} %bitcast.4, bf16[8,1280]{1,0:T(8,128)(2,1)} %temb.1, bf16[1280,320]{1,0:T(8,128)(2,1)} %copy.14.tw, f32[1,320]{1,0:T(1,128)} %reshape.35.gain1, f32[1,320]{1,0:T(1,128)} %reshape.36.shift1, ...), custom_call_target="tpu_custom_call" | custom-call | tf_op jit(solution)/shard_map/block/pallas_call | solution.py:331
  73.0 6.5 %finish.1 = (bf16[8,1280,128]{2,1,0:T(8,128)(2,1)}, bf16[1,320,256]{2,1,0:T(8,128)(2,1)}) custom-call(bf16[8,4,320,128]{3,2,1,0:T(8,128)(2,1)} %get-tuple-element.6.res, bf16[32,16,256]{2,1,0:T(8,128)(2,1)} %get-tuple-element.7.tok), custom_call_target="tpu_custom_call" | custom-call | tf_op jit(solution)/shard_map/finish/pallas_call | solution.py:378

commit v2 on v1

v2 whole, which is shorter than its diff:
```python
import functools

import jax
import jax.numpy as jnp
from jax import lax
from jax.experimental import pallas as pl
from jax.experimental.pallas import tpu as pltpu
from jax.sharding import PartitionSpec as P

F32 = jnp.float32
BF16 = jnp.bfloat16
C = 320
GROUPS = 32
PER = C // GROUPS
W = 128
TEMB = 1280
R = 4
FR = 8
ND = 32
FG = 4
DEPTH = 3 * C + 32
MESH = pl.DeviceIdType.MESH


def dot(a, b):
    return jnp.dot(a, b, preferred_element_type=F32)


def dot_nt(a, b):
    return lax.dot_general(a, b, (((1,), (1,)), ((), ())), preferred_element_type=F32)


def to_row(x):
    return jnp.sum(jnp.transpose(x), axis=0, keepdims=True)


def to_cols(row):
    return jnp.transpose(jnp.broadcast_to(row, (W, C)))


def split3(a):
    high = a.astype(BF16)
    rest = a - high.astype(F32)
    mid = rest.astype(BF16)
    return jnp.concatenate([high, mid, (rest - mid.astype(F32)).astype(BF16)], axis=0)


def exact(a, ones):
    m = a.shape[0]
    y = dot(split3(a), ones)
    return y[0:m] + y[m : 2 * m] + y[2 * m : 3 * m]


def group_of(shape, dim):
    i = lax.broadcasted_iota(jnp.int32, shape, dim)
    return lax.div(i, PER)


def where_one(flags):
    return jnp.where(flags, 1.0, 0.0).astype(BF16)


def place_weights(raw, packed, offsets):
    parts = split3(offsets).astype(F32)
    parts = jnp.transpose(jnp.concatenate([parts, jnp.zeros((W - 24, C), F32)], axis=0))
    parts = parts[:, 0:32].astype(BF16)
    for b in range(3):
        rows = slice(b * C, (b + 1) * C)
        for a in range(3):
            packed[rows, a * 256 : (a + 1) * 256] = raw[a * 3 + b, :, 0:256]
        rest = [raw[a * 3 + b, :, 256:C] for a in range(3)]
        rest.append(parts if b == 1 else jnp.zeros((C, 32), BF16))
        packed[rows, 768:DEPTH] = jnp.concatenate(rest, axis=1)


def conv_half(act, packed, f, half):
    lane = lax.broadcasted_iota(jnp.int32, (C, W), 1)
    row = lax.broadcasted_iota(jnp.int32, (32, 2 * W), 0)
    mine = where_one((lax.rem(row, 8) == f) & (row < 24))
    at = [slice((half * 2 + a) * W, (half * 2 + a) * W + 2 * W) for a in range(3)]
    rhs = jnp.concatenate(
        [act[0:256, at[a]] for a in range(3)] + [act[256:C, at[a]] for a in range(3)] + [mine], axis=0
    )
    y = [dot(packed[b * C : (b + 1) * C, :], rhs) for b in range(3)]
    rows = []
    for r in range(2):
        s = slice(r * W, (r + 1) * W)
        left = jnp.where(lane == 0, 0.0, pltpu.roll(y[0][:, s], 1, 1))
        right = jnp.where(lane == W - 1, 0.0, pltpu.roll(y[2][:, s], W - 1, 1))
        rows.append(y[1][:, s] + left + right)
    return rows


def main_kernel(
    lat_in, temb_in, tw_in, gain1_in, shift1_in, w1_in, bias1_in, gain2_in, shift2_in, w2_in, bias2_in, order_in,
    res, tok,
    lraw, temb, tw, gain1, shift1, raw1, bias1, gain2, shift2, raw2, bias2, order,
    wide, wide2, x6, h6, act0, act1, pk1, pk2, resbuf, obuf, sums,
    means, sqs, gath, msg, coef, same, lanes_a, lanes_b, rows_g, orders, chosen, tsend, trecv,
    in_sem, small_sem, out_sem, halo_send, halo_recv, ag_send, ag_recv, tok_send, tok_recv,
):
    clip, me = lax.axis_index("clip"), lax.axis_index("rows")
    up, down = lax.rem(me + ND - 1, ND), lax.rem(me + 1, ND)
    n_local = float(PER * R * W)

    def partner(k):
        return lax.rem(me + k, ND)

    fetch = [pltpu.make_async_copy(lat_in.at[f], lraw.at[f], in_sem.at[f]) for f in range(FR)]
    for copy in fetch:
        copy.start()

    barrier = pltpu.get_barrier_semaphore()

    def greet(k, carry):
        pl.semaphore_signal(barrier, inc=1, device_id=(clip, partner(k)), device_id_type=MESH)
        return carry

    lax.fori_loop(1, ND, greet, 0)

    others = [
        (temb_in, temb), (tw_in, tw), (bias1_in, bias1), (w1_in, raw1), (gain1_in, gain1), (shift1_in, shift1),
        (bias2_in, bias2), (w2_in, raw2), (gain2_in, gain2), (shift2_in, shift2), (order_in, order),
    ]
    others = [pltpu.make_async_copy(a, b, small_sem.at[i]) for i, (a, b) in enumerate(others)]

    def halo_copies(stage, pair):
        buf = (x6, h6)[stage]
        frames = pl.ds(pair * 2, 2)
        return [
            pltpu.make_async_remote_copy(
                src_ref=buf.at[src, frames], dst_ref=buf.at[dst, frames],
                send_sem=halo_send.at[stage, pair, i], recv_sem=halo_recv.at[stage, pair, i],
                device_id=(clip, to), device_id_type=MESH,
            )
            for i, (src, dst, to) in enumerate(((1, 5, up), (4, 0, down)))
        ]

    def halo_start(stage, pair):
        for copy in halo_copies(stage, pair):
            copy.start()

    def halo_wait(stage, pair):
        for copy in halo_copies(stage, pair):
            copy.wait()

    def ag_copy(slot, k):
        return pltpu.make_async_remote_copy(
            src_ref=msg.at[slot], dst_ref=gath.at[slot, me],
            send_sem=ag_send.at[slot, k], recv_sem=ag_recv.at[slot, k],
            device_id=(clip, partner(k)), device_id_type=MESH,
        )

    def gather_start(slot):
        for k in range(1, ND):
            ag_copy(slot, k).start()
        gath[slot, me] = msg[slot]

    def gather_end(slot):
        def one(k, carry):
            ag_copy(slot, k).wait()
            return carry

        lax.fori_loop(1, ND, one, 0)
        every = gath[slot]
        lane = lax.broadcasted_iota(jnp.int32, (8, W), 1)
        total = jnp.sum(every, axis=0)
        mean = total * (1.0 / ND)
        away = every - mean[None]
        spread = jnp.sum(away * away, axis=0) * n_local
        square = total + pltpu.roll(spread, GROUPS, 1)
        return jnp.where(lane < GROUPS, mean, jnp.where(lane < 2 * GROUPS, square, 0.0))

    def channel_stats(j, xs):
        total = (xs[0] + xs[1]) + (xs[2] + xs[3])
        middle = total * (1.0 / R)
        away = None
        for x in xs:
            d = x - middle
            away = d * d if away is None else away + d * d
        mean = to_row(total) * (1.0 / (R * W))
        d = middle - to_cols(mean)
        means[pl.ds(j, 1), :] = mean
        sqs[pl.ds(j, 1), :] = to_row(away + d * d * float(R))

    def channel_sums(j, xs):
        total = (xs[0] + xs[1]) + (xs[2] + xs[3])
        square = (xs[0] * xs[0] + xs[1] * xs[1]) + (xs[2] * xs[2] + xs[3] * xs[3])
        mean = to_row(total) * (1.0 / (R * W))
        means[pl.ds(j, 1), :] = mean
        sqs[pl.ds(j, 1), :] = to_row(square) - mean * mean * float(R * W)

    def stats(slot):
        mean = means[...]
        d = mean - exact(mean, same[...]) * (1.0 / PER)
        inner = sqs[...] + d * d * float(R * W)
        msg[slot] = exact(mean, lanes_a[...]) * (1.0 / PER) + exact(inner, lanes_b[...])

    def coefs(slot, gain, shift):
        both = gather_end(slot)
        valid = lax.broadcasted_iota(jnp.int32, (8, W), 1) < GROUPS
        var = jnp.maximum(pltpu.roll(both, W - GROUPS, 1), 0.0) * (1.0 / (ND * n_local))
        inv = jnp.where(valid, lax.rsqrt(var + 1e-5), 0.0)
        both = exact(jnp.concatenate([inv, jnp.where(valid, both, 0.0)], axis=0), rows_g[...])
        scale = both[0:8] * gain[...].reshape(1, C)
        coef[0] = scale * 0.5
        coef[1] = (shift[...].reshape(1, C) - both[8:16] * scale) * 0.5

    def activate(buf, act, f, j):
        sc = to_cols(coef[0, pl.ds(j, 1), :])
        sh = to_cols(coef[1, pl.ds(j, 1), :])
        for row in range(R + 2):
            h = buf[row, f].astype(F32) * sc + sh
            a = h * jnp.tanh(h) + h
            if row == 0:
                a = jnp.where(me > 0, a, 0.0)
            if row == R + 1:
                a = jnp.where(me < ND - 1, a, 0.0)
            act[:, row * W : (row + 1) * W] = a.astype(BF16)

    acts = (act0, act1)

    def split(i, carry):
        for p, buf in enumerate((wide, wide2)):
            f = i * 2 + p
            pltpu.make_async_copy(lat_in.at[f], lraw.at[f], in_sem.at[f]).wait()
        for p, buf in enumerate((wide, wide2)):
            f = i * 2 + p
            buf[...] = lraw[f].astype(F32)
            xs = [buf[pl.ds(r, C, stride=R), :] for r in range(R)]
            for r in range(R):
                x6[r + 1, f] = xs[r].astype(BF16)
            channel_stats(f, xs)
        return carry

    lax.fori_loop(0, 1, split, 0)
    pl.semaphore_wait(barrier, ND - 1)
    halo_start(0, 0)
    lax.fori_loop(1, FR // 2, split, 0)
    for copy in others:
        copy.start()
    same[...] = where_one(group_of((C, C), 0) == group_of((C, C), 1))
    lane = lax.broadcasted_iota(jnp.int32, (C, W), 1)
    lanes_a[...] = where_one(group_of((C, W), 0) == lane)
    lanes_b[...] = where_one(group_of((C, W), 0) + GROUPS == lane)
    stats(0)
    gather_start(0)
    for pair in range(1, FR // 2):
        halo_start(0, pair)

    rows_g[...] = where_one(group_of((W, C), 1) == lax.broadcasted_iota(jnp.int32, (W, C), 0))
    for copy in others:
        copy.wait()
    embed = temb[...].astype(F32)
    tact = (embed / (1.0 + jnp.exp(-embed))).astype(BF16)
    place_weights(raw1, pk1, dot_nt(tact, tw[...]) + bias1[...].reshape(1, C))
    place_weights(raw2, pk2, jnp.broadcast_to(bias2[...].reshape(1, C), (8, C)))
    orders[...] = jnp.transpose(jnp.broadcast_to(order[...].astype(F32), (2 * W, 256))).astype(jnp.int32)
    chosen[...] = jnp.zeros((256, C), F32)

    coefs(0, gain1, shift1)
    halo_wait(0, 0)
    activate(x6, act0, 0, 0)
    for f in range(FR):
        if f + 1 < FR:
            if f % 2 == 1:
                halo_wait(0, (f + 1) // 2)
            activate(x6, acts[(f + 1) % 2], f + 1, f + 1)
        xs = []
        for half in range(2):
            for y in conv_half(acts[f % 2], pk1, f, half):
                h = y.astype(BF16)
                h6[len(xs) + 1, f] = h
                xs.append(h.astype(F32))
        channel_sums(f % FG, xs)
        if f == FG - 1:
            stats(1)
            gather_start(1)
        if f % 2 == 1 and f < FR - 1:
            halo_start(1, f // 2)
    stats(2)

    quarter = lax.div(lax.broadcasted_iota(jnp.int32, (256, 2 * W), 1), 4)
    coefs(1, gain2, shift2)
    halo_wait(1, 0)
    gather_start(2)
    halo_start(1, FR // 2 - 1)
    activate(h6, act0, 0, 0)
    for f in range(FR):
        if f + 1 < FR:
            if f + 1 == FG:
                coefs(2, gain2, shift2)
            if f % 2 == 1:
                halo_wait(1, (f + 1) // 2)
            activate(h6, acts[(f + 1) % 2], f + 1, (f + 1) % FG)
        total = None
        for half in range(2):
            for i, y in enumerate(conv_half(acts[f % 2], pk2, f, half)):
                r = half * 2 + i
                v = y + x6[r + 1, f].astype(F32)
                resbuf[f, r] = v.astype(BF16)
                total = v if total is None else total + v
        high = total.astype(BF16)
        cols = slice(f % 2 * W, f % 2 * W + W)
        sums[0, :, cols] = high
        sums[1, :, cols] = (total - high.astype(F32)).astype(BF16)
        if f % 2 == 1:
            pick = jnp.where(orders[...] == quarter + f // 2 * (W // 2), 1.0 / 16.0, 0.0).astype(BF16)
            chosen[...] += dot_nt(pick, sums[0]) + dot_nt(pick, sums[1])

    placed = chosen[...].reshape(ND, 8, C)
    lower = jnp.concatenate([placed[:, :, 256:C], jnp.zeros((ND, 8, 512 - C), F32)], axis=2)
    tsend[...] = jnp.concatenate([placed[:, :, 0:256], lower], axis=1).astype(BF16)

    def tok_copy(k):
        return pltpu.make_async_remote_copy(
            src_ref=tsend.at[partner(k)], dst_ref=trecv.at[me],
            send_sem=tok_send.at[k], recv_sem=tok_recv.at[k],
            device_id=(clip, partner(k)), device_id_type=MESH,
        )

    def tok_wait(k, carry):
        tok_copy(k).wait()
        return carry

    for k in range(1, ND):
        tok_copy(k).start()
    trecv[me] = tsend[me]

    def put(f):
        return pltpu.make_async_copy(obuf.at[f], res.at[f], out_sem.at[f])

    for f in range(FR):
        buf = (wide, wide2)[f % 2]
        for r in range(R):
            buf[pl.ds(r, C, stride=R), :] = resbuf[f, r].astype(F32)
        obuf[f] = buf[...].astype(BF16)
        put(f).start()

    lax.fori_loop(1, ND, tok_wait, 0)
    last = pltpu.make_async_copy(trecv, tok, small_sem.at[0])
    last.start()
    for f in range(FR):
        put(f).wait()
    last.wait()


def finish_kernel(res, tok, out, student, rbuf, tbuf, sbuf, in_sem, out_sem):
    fetch = [pltpu.make_async_copy(res.at[f], rbuf.at[f], in_sem.at[f]) for f in range(FR)]
    put = [pltpu.make_async_copy(rbuf.at[f], out.at[f], out_sem.at[f]) for f in range(FR)]
    tokens = pltpu.make_async_copy(tok, tbuf, in_sem.at[FR])
    for copy in fetch:
        copy.start()
    tokens.start()
    for f in range(FR // 2):
        fetch[f].wait()
        put[f].start()
    tokens.wait()
    t = tbuf[...].astype(F32)
    top = jnp.transpose(t[:, 0:8, :].reshape(256, 256))
    low = jnp.transpose(t[:, 8:16, 0:128].reshape(256, 128))
    sbuf[...] = jnp.concatenate([top, low[0 : C - 256]], axis=0).astype(BF16)
    put.append(pltpu.make_async_copy(sbuf, student.at[0], out_sem.at[FR]))
    put[FR].start()
    for f in range(FR // 2, FR):
        fetch[f].wait()
        put[f].start()
    for copy in put:
        copy.wait()


def body(lat, temb, tw, gain1, shift1, w1, bias1, gain2, shift2, w2, bias2, order):
    anyspace = pl.BlockSpec(memory_space=pl.ANY)
    dma = pltpu.SemaphoreType.DMA
    vec = pltpu.VMEM((C,), F32)
    raw = pltpu.VMEM((9, C, C), BF16)
    pairs = dma((2, FR // 2, 2))
    res, tok = pl.pallas_call(
        main_kernel,
        out_shape=(
            jax.ShapeDtypeStruct((FR, C * R, W), BF16),
            jax.ShapeDtypeStruct((ND, 16, 256), BF16),
        ),
        in_specs=[anyspace] * 12,
        out_specs=(anyspace, anyspace),
        scratch_shapes=[
            pltpu.VMEM((FR, C * R, W), BF16),
            pltpu.VMEM((FR, TEMB), BF16),
            pltpu.VMEM((C, TEMB), BF16),
            vec, vec, raw, vec, vec, vec, raw, vec,
            pltpu.VMEM((1, 256), jnp.int32),
            pltpu.VMEM((C * R, W), F32),
            pltpu.VMEM((C * R, W), F32),
            pltpu.VMEM((R + 2, FR, C, W), BF16),
            pltpu.VMEM((R + 2, FR, C, W), BF16),
            pltpu.VMEM((C, (R + 2) * W), BF16),
            pltpu.VMEM((C, (R + 2) * W), BF16),
            pltpu.VMEM((3 * C, DEPTH), BF16),
            pltpu.VMEM((3 * C, DEPTH), BF16),
            pltpu.VMEM((FR, R, C, W), BF16),
            pltpu.VMEM((FR, C * R, W), BF16),
            pltpu.VMEM((2, C, 2 * W), BF16),
            pltpu.VMEM((8, C), F32),
            pltpu.VMEM((8, C), F32),
            pltpu.VMEM((3, ND, 8, W), F32),
            pltpu.VMEM((3, 8, W), F32),
            pltpu.VMEM((2, 8, C), F32),
            pltpu.VMEM((C, C), BF16),
            pltpu.VMEM((C, W), BF16),
            pltpu.VMEM((C, W), BF16),
            pltpu.VMEM((W, C), BF16),
            pltpu.VMEM((256, 2 * W), jnp.int32),
            pltpu.VMEM((256, C), F32),
            pltpu.VMEM((ND, 16, 256), BF16),
            pltpu.VMEM((ND, 16, 256), BF16),
            dma((FR,)), dma((11,)), dma((FR,)), pairs, pairs,
            dma((3, ND)), dma((3, ND)), dma((ND,)), dma((ND,)),
        ],
        compiler_params=pltpu.CompilerParams(
            collective_id=0, has_side_effects=True, vmem_limit_bytes=56 * 2**20
        ),
        name="block",
    )(
        lat.reshape(FR, C * R, W), temb, tw.T, gain1, shift1, w1.reshape(9, C, C), bias1,
        gain2, shift2, w2.reshape(9, C, C), bias2, order,
    )
    out, student = pl.pallas_call(
        finish_kernel,
        out_shape=(
            jax.ShapeDtypeStruct((FR, C * R, W), BF16),
            jax.ShapeDtypeStruct((1, C, 256), BF16),
        ),
        in_specs=[anyspace, anyspace],
        out_specs=(anyspace, anyspace),
        scratch_shapes=[
            pltpu.VMEM((FR, C * R, W), BF16),
            pltpu.VMEM((ND, 16, 256), BF16),
            pltpu.VMEM((C, 256), BF16),
            dma((FR + 1,)),
            dma((FR + 1,)),
        ],
        compiler_params=pltpu.CompilerParams(vmem_limit_bytes=56 * 2**20),
        name="finish",
    )(res, tok)
    return out.reshape(FR, C, R, W), student


def solution(mesh):
    return jax.shard_map(
        body,
        mesh=mesh,
        in_specs=(
            P("clip", None, "rows", None),
            P("clip", None),
            P(), P(), P(), P(), P(), P(), P(), P(), P(),
            P("clip", "rows"),
        ),
        out_specs=(P("clip", None, "rows", None), P("clip", None, "rows")),
        check_vma=False,
    )
```

time: 79.9 us -> 57.2 us (0.72)
  Pallas kernels: 69.2 us -> 56.2 us
  local copies, waits for them, and re-layouts: 9.61 us -> 0 us
    pallas_call x2, Pallas kernels: 69.2 us -> 56.2 us  [the longest x1 53.1 us: body(): pl.pallas_call(main_kernel, out_shape=(jax.ShapeDtypeStruct((FR, C * R, W...]
    reshape x6 -> x0, local copies, waits for them, and re-layouts: 7.41 us -> none  [body(): row = lambda v: v.reshape(1, C)]
    unnamed x1 -> x0, local copies, waits for them, and re-layouts: 2.2 us -> none
where the time goes in v2:
time: 57.2 us; the launch traced here: 57 us
  Pallas kernels  56.2 us (98%)
  between operations  0.82 us (1%)
    pallas_call x1, Pallas kernels, body(): pl.pallas_call(main_kernel, out_shape=(jax.ShapeDtypeStruct((FR, C * R, W...  53.1 us
    pallas_call x1, Pallas kernels, body(): pl.pallas_call(finish_kernel, out_shape=(jax.ShapeDtypeStruct((FR, C * R,...  3.12 us

profile of v2, /device:TPU:1, one launch (start us, length us, event | category | flops | bytes accessed | tf_op | source)
XLA Modules:
  0.0 57.0 jit_solution(8873176305923856390)
XLA Ops:
  0.6 53.1 %block.1 = (bf16[8,1280,128]{2,1,0:T(8,128)(2,1)}, bf16[32,16,256]{2,1,0:T(8,128)(2,1)}) custom-call(bf16[8,1280,128]{2,1,0:T(8,128)(2,1)} %bitcast.5, bf16[8,1280]{1,0:T(8,128)(2,1)} %temb_in.1, bf16[320,1280]{1,0:T(8,128)(2,1)} %bitcast.8, f32[320]{0:T(512)} %gain1_in.1, f32[320]{0:T(512)} %shift1_in.1, bf16[9,320,320]{2,1,0:T(8,128)(2,1)} %bitcast.6, ...), custom_call_target="tpu_custom_call" | custom-call | tf_op jit(solution)/shard_map/block/pallas_call | solution.py:378
  53.7 3.1 %finish.1 = (bf16[8,1280,128]{2,1,0:T(8,128)(2,1)}, bf16[1,320,256]{2,1,0:T(8,128)(2,1)}) custom-call(bf16[8,1280,128]{2,1,0:T(8,128)(2,1)} %get-tuple-element.6.res, bf16[32,16,256]{2,1,0:T(8,128)(2,1)} %get-tuple-element.7.tok), custom_call_target="tpu_custom_call" | custom-call | tf_op jit(solution)/shard_map/finish/pallas_call | solution.py:427

commit v3 on v2

--- a/solution.py
+++ b/solution.py
@@ -17,7 +17,9 @@
 R = 4
 FR = 8
 ND = 32
-FG = 4
+EDGES = (((0, 2), (2, 1), (3, 2), (5, 2), (7, 1)), ((0, 2), (2, 2), (4, 2), (6, 2)))
+SLOT_TWO = (1, 1, 1, 1, 2, 2, 3, 3)
+SLOTS = 4
 DEPTH = 3 * C + 32
 MESH = pl.DeviceIdType.MESH
 
@@ -95,9 +97,9 @@
     lat_in, temb_in, tw_in, gain1_in, shift1_in, w1_in, bias1_in, gain2_in, shift2_in, w2_in, bias2_in, order_in,
     res, tok,
     lraw, temb, tw, gain1, shift1, raw1, bias1, gain2, shift2, raw2, bias2, order,
-    wide, wide2, x6, h6, act0, act1, pk1, pk2, resbuf, obuf, sums,
+    wide, wide2, x6, h6, act0, act1, pk1, pk2, resbuf, sums,
     means, sqs, gath, msg, coef, same, lanes_a, lanes_b, rows_g, orders, chosen, tsend, trecv,
-    in_sem, small_sem, out_sem, halo_send, halo_recv, ag_send, ag_recv, tok_send, tok_recv,
+    in_sem, small_sem, halo_send, halo_recv, ag_send, ag_recv, tok_send, tok_recv,
 ):
     clip, me = lax.axis_index("clip"), lax.axis_index("rows")
     up, down = lax.rem(me + ND - 1, ND), lax.rem(me + 1, ND)
@@ -124,24 +126,24 @@
     ]
     others = [pltpu.make_async_copy(a, b, small_sem.at[i]) for i, (a, b) in enumerate(others)]
 
-    def halo_copies(stage, pair):
+    def halo_copies(stage, n):
         buf = (x6, h6)[stage]
-        frames = pl.ds(pair * 2, 2)
+        frames = pl.ds(*EDGES[stage][n])
         return [
             pltpu.make_async_remote_copy(
                 src_ref=buf.at[src, frames], dst_ref=buf.at[dst, frames],
-                send_sem=halo_send.at[stage, pair, i], recv_sem=halo_recv.at[stage, pair, i],
+                send_sem=halo_send.at[stage, n, i], recv_sem=halo_recv.at[stage, n, i],
                 device_id=(clip, to), device_id_type=MESH,
             )
             for i, (src, dst, to) in enumerate(((1, 5, up), (4, 0, down)))
         ]
 
-    def halo_start(stage, pair):
-        for copy in halo_copies(stage, pair):
+    def halo_start(stage, n):
+        for copy in halo_copies(stage, n):
             copy.start()
 
-    def halo_wait(stage, pair):
-        for copy in halo_copies(stage, pair):
+    def halo_wait(stage, n):
+        for copy in halo_copies(stage, n):
             copy.wait()
 
     def ag_copy(slot, k):
@@ -152,9 +154,9 @@
         )
 
     def gather_start(slot):
+        gath[slot, me] = msg[slot]
         for k in range(1, ND):
             ag_copy(slot, k).start()
-        gath[slot, me] = msg[slot]
 
     def gather_end(slot):
         def one(k, carry):
@@ -203,12 +205,12 @@
         inv = jnp.where(valid, lax.rsqrt(var + 1e-5), 0.0)
         both = exact(jnp.concatenate([inv, jnp.where(valid, both, 0.0)], axis=0), rows_g[...])
         scale = both[0:8] * gain[...].reshape(1, C)
-        coef[0] = scale * 0.5
-        coef[1] = (shift[...].reshape(1, C) - both[8:16] * scale) * 0.5
-
-    def activate(buf, act, f, j):
-        sc = to_cols(coef[0, pl.ds(j, 1), :])
-        sh = to_cols(coef[1, pl.ds(j, 1), :])
+        coef[slot, 0] = scale * 0.5
+        coef[slot, 1] = (shift[...].reshape(1, C) - both[8:16] * scale) * 0.5
+
+    def activate(buf, act, slot, f):
+        sc = to_cols(coef[slot, 0, pl.ds(f, 1), :])
+        sh = to_cols(coef[slot, 1, pl.ds(f, 1), :])
         for row in range(R + 2):
             h = buf[row, f].astype(F32) * sc + sh
             a = h * jnp.tanh(h) + h
@@ -233,6 +235,8 @@
             channel_stats(f, xs)
         return carry
 
+    means[...] = jnp.zeros((8, C), F32)
+    sqs[...] = jnp.zeros((8, C), F32)
     lax.fori_loop(0, 1, split, 0)
     pl.semaphore_wait(barrier, ND - 1)
     halo_start(0, 0)
@@ -245,8 +249,8 @@
     lanes_b[...] = where_one(group_of((C, W), 0) + GROUPS == lane)
     stats(0)
     gather_start(0)
-    for pair in range(1, FR // 2):
-        halo_start(0, pair)
+    for n in range(1, len(EDGES[0])):
+        halo_start(0, n)
 
     rows_g[...] = where_one(group_of((W, C), 1) == lax.broadcasted_iota(jnp.int32, (W, C), 0))
     for copy in others:
@@ -260,39 +264,40 @@
 
     coefs(0, gain1, shift1)
     halo_wait(0, 0)
+    halo_wait(0, 1)
     activate(x6, act0, 0, 0)
     for f in range(FR):
+        if f in (2, 4, 6):
+            if f > 2:
+                stats(SLOT_TWO[f - 1])
+                gather_start(SLOT_TWO[f - 1])
+            halo_wait(0, f // 2 + 1)
+            halo_start(1, f // 2 - 1)
         if f + 1 < FR:
-            if f % 2 == 1:
-                halo_wait(0, (f + 1) // 2)
-            activate(x6, acts[(f + 1) % 2], f + 1, f + 1)
+            activate(x6, acts[(f + 1) % 2], 0, f + 1)
         xs = []
         for half in range(2):
             for y in conv_half(acts[f % 2], pk1, f, half):
                 h = y.astype(BF16)
                 h6[len(xs) + 1, f] = h
                 xs.append(h.astype(F32))
-        channel_sums(f % FG, xs)
-        if f == FG - 1:
-            stats(1)
-            gather_start(1)
-        if f % 2 == 1 and f < FR - 1:
-            halo_start(1, f // 2)
-    stats(2)
+        channel_sums(f, xs)
+    stats(SLOT_TWO[FR - 1])
 
     quarter = lax.div(lax.broadcasted_iota(jnp.int32, (256, 2 * W), 1), 4)
     coefs(1, gain2, shift2)
     halo_wait(1, 0)
-    gather_start(2)
+    gather_start(SLOT_TWO[FR - 1])
     halo_start(1, FR // 2 - 1)
-    activate(h6, act0, 0, 0)
+    activate(h6, act0, 1, 0)
     for f in range(FR):
         if f + 1 < FR:
-            if f + 1 == FG:
-                coefs(2, gain2, shift2)
+            slot = SLOT_TWO[f + 1]
+            if SLOT_TWO[f] != slot:
+                coefs(slot, gain2, shift2)
             if f % 2 == 1:
                 halo_wait(1, (f + 1) // 2)
-            activate(h6, acts[(f + 1) % 2], f + 1, (f + 1) % FG)
+            activate(h6, acts[(f + 1) % 2], slot, f + 1)
         total = None
         for half in range(2):
             for i, y in enumerate(conv_half(acts[f % 2], pk2, f, half)):
@@ -327,62 +332,45 @@
         tok_copy(k).start()
     trecv[me] = tsend[me]
 
-    def put(f):
-        return pltpu.make_async_copy(obuf.at[f], res.at[f], out_sem.at[f])
-
     for f in range(FR):
         buf = (wide, wide2)[f % 2]
         for r in range(R):
             buf[pl.ds(r, C, stride=R), :] = resbuf[f, r].astype(F32)
-        obuf[f] = buf[...].astype(BF16)
-        put(f).start()
+        res[f] = buf[...].astype(BF16)
 
     lax.fori_loop(1, ND, tok_wait, 0)
-    last = pltpu.make_async_copy(trecv, tok, small_sem.at[0])
-    last.start()
-    for f in range(FR):
-        put(f).wait()
-    last.wait()
-
-
-def finish_kernel(res, tok, out, student, rbuf, tbuf, sbuf, in_sem, out_sem):
-    fetch = [pltpu.make_async_copy(res.at[f], rbuf.at[f], in_sem.at[f]) for f in range(FR)]
-    put = [pltpu.make_async_copy(rbuf.at[f], out.at[f], out_sem.at[f]) for f in range(FR)]
-    tokens = pltpu.make_async_copy(tok, tbuf, in_sem.at[FR])
-    for copy in fetch:
+    tok[...] = trecv[...]
+
+
+def finish_kernel(res, tok, out, student, sbuf, sem):
+    put = [pltpu.make_async_copy(res.at[f], out.at[f], sem.at[f]) for f in range(FR)]
+    for copy in put:
         copy.start()
-    tokens.start()
-    for f in range(FR // 2):
-        fetch[f].wait()
-        put[f].start()
-    tokens.wait()
-    t = tbuf[...].astype(F32)
+    t = tok[...].astype(F32)
     top = jnp.transpose(t[:, 0:8, :].reshape(256, 256))
     low = jnp.transpose(t[:, 8:16, 0:128].reshape(256, 128))
     sbuf[...] = jnp.concatenate([top, low[0 : C - 256]], axis=0).astype(BF16)
-    put.append(pltpu.make_async_copy(sbuf, student.at[0], out_sem.at[FR]))
+    put.append(pltpu.make_async_copy(sbuf, student.at[0], sem.at[FR]))
     put[FR].start()
-    for f in range(FR // 2, FR):
-        fetch[f].wait()
-        put[f].start()
     for copy in put:
         copy.wait()
 
 
 def body(lat, temb, tw, gain1, shift1, w1, bias1, gain2, shift2, w2, bias2, order):
     anyspace = pl.BlockSpec(memory_space=pl.ANY)
+    vm = pl.BlockSpec(memory_space=pltpu.VMEM)
     dma = pltpu.SemaphoreType.DMA
     vec = pltpu.VMEM((C,), F32)
     raw = pltpu.VMEM((9, C, C), BF16)
-    pairs = dma((2, FR // 2, 2))
+    edges = dma((2, len(EDGES[0]), 2))
     res, tok = pl.pallas_call(
         main_kernel,
         out_shape=(
-            jax.ShapeDtypeStruct((FR, C * R, W), BF16),
-            jax.ShapeDtypeStruct((ND, 16, 256), BF16),
+            pltpu.VMEM((FR, C * R, W), BF16),
+            pltpu.VMEM((ND, 16, 256), BF16),
         ),
-        in_specs=[anyspace] * 12,
-        out_specs=(anyspace, anyspace),
+        in_specs=[pl.BlockSpec(memory_space=pltpu.HBM)] * 12,
+        out_specs=(vm, vm),
         scratch_shapes=[
             pltpu.VMEM((FR, C * R, W), BF16),
             pltpu.VMEM((FR, TEMB), BF16),
@@ -398,13 +386,12 @@
             pltpu.VMEM((3 * C, DEPTH), BF16),
             pltpu.VMEM((3 * C, DEPTH), BF16),
             pltpu.VMEM((FR, R, C, W), BF16),
-            pltpu.VMEM((FR, C * R, W), BF16),
             pltpu.VMEM((2, C, 2 * W), BF16),
             pltpu.VMEM((8, C), F32),
             pltpu.VMEM((8, C), F32),
-            pltpu.VMEM((3, ND, 8, W), F32),
-            pltpu.VMEM((3, 8, W), F32),
-            pltpu.VMEM((2, 8, C), F32),
+            pltpu.VMEM((SLOTS, ND, 8, W), F32),
+            pltpu.VMEM((SLOTS, 8, W), F32),
+            pltpu.VMEM((SLOTS, 2, 8, C), F32),
             pltpu.VMEM((C, C), BF16),
             pltpu.VMEM((C, W), BF16),
             pltpu.VMEM((C, W), BF16),
@@ -413,16 +400,21 @@
             pltpu.VMEM((256, C), F32),
             pltpu.VMEM((ND, 16, 256), BF16),
             pltpu.VMEM((ND, 16, 256), BF16),
-            dma((FR,)), dma((11,)), dma((FR,)), pairs, pairs,
-            dma((3, ND)), dma((3, ND)), dma((ND,)), dma((ND,)),
+            dma((FR,)), dma((11,)), edges, edges,
+            dma((SLOTS, ND)), dma((SLOTS, ND)), dma((ND,)), dma((ND,)),
         ],
         compiler_params=pltpu.CompilerParams(
             collective_id=0, has_side_effects=True, vmem_limit_bytes=56 * 2**20
         ),
         name="block",
     )(
-        lat.reshape(FR, C * R, W), temb, tw.T, gain1, shift1, w1.reshape(9, C, C), bias1,
-        gain2, shift2, w2.reshape(9, C, C), bias2, order,
+        *(
+            pltpu.with_memory_space_constraint(a, pltpu.HBM)
+            for a in (
+                lat.reshape(FR, C * R, W), temb, tw.T, gain1, shift1, w1.reshape(9, C, C), bias1,
+                gain2, shift2, w2.reshape(9, C, C), bias2, order,
+            )
+        )
     )
     out, student = pl.pallas_call(
         finish_kernel,
@@ -430,18 +422,15 @@
             jax.ShapeDtypeStruct((FR, C * R, W), BF16),
             jax.ShapeDtypeStruct((1, C, 256), BF16),
         ),
-        in_specs=[anyspace, anyspace],
+        in_specs=[vm, vm],
         out_specs=(anyspace, anyspace),
-        scratch_shapes=[
-            pltpu.VMEM((FR, C * R, W), BF16),
-            pltpu.VMEM((ND, 16, 256), BF16),
-            pltpu.VMEM((C, 256), BF16),
-            dma((FR + 1,)),
-            dma((FR + 1,)),
-        ],
-        compiler_params=pltpu.CompilerParams(vmem_limit_bytes=56 * 2**20),
+        scratch_shapes=[pltpu.VMEM((C, 256), BF16), dma((FR + 1,))],
+        compiler_params=pltpu.CompilerParams(vmem_limit_bytes=16 * 2**20),
         name="finish",
-    )(res, tok)
+    )(
+        pltpu.with_memory_space_constraint(res, pltpu.VMEM),
+        pltpu.with_memory_space_constraint(tok, pltpu.VMEM),
+    )
     return out.reshape(FR, C, R, W), student
 
 

time: 57.2 us -> 55.3 us (0.967)
  Pallas kernels: 56.2 us -> 54.3 us
    pallas_call x1, Pallas kernels: 3.12 us -> 1.61 us  [body(): pl.pallas_call(finish_kernel, out_shape=(jax.ShapeDtypeStruct((FR, C * R,...]
where the time goes in v3:
time: 55.3 us; the launch traced here: 55.1 us
  Pallas kernels  54.3 us (98%)
  between operations  0.82 us (1%)
    pallas_call x1, Pallas kernels, body(): pl.pallas_call(main_kernel, out_shape=(pltpu.VMEM((FR, C * R, W), BF16),...  52.7 us
    pallas_call x1, Pallas kernels, body(): pl.pallas_call(finish_kernel, out_shape=(jax.ShapeDtypeStruct((FR, C * R,...  1.61 us

profile of v3, /device:TPU:1, one launch (start us, length us, event | category | flops | bytes accessed | tf_op | source)
XLA Modules:
  0.0 55.1 jit_solution(6783037168055182298)
XLA Ops:
  0.6 52.7 %block.1 = (bf16[8,1280,128]{2,1,0:T(8,128)(2,1)S(1)}, bf16[32,16,256]{2,1,0:T(8,128)(2,1)S(1)}) custom-call(bf16[8,1280,128]{2,1,0:T(8,128)(2,1)} %bitcast.5, bf16[8,1280]{1,0:T(8,128)(2,1)} %temb_in.1, bf16[320,1280]{1,0:T(8,128)(2,1)} %bitcast.8, f32[320]{0:T(512)} %gain1_in.1, f32[320]{0:T(512)} %shift1_in.1, bf16[9,320,320]{2,1,0:T(8,128)(2,1)} %bitcast.6, ...), custom_call_target="tpu_custom_call" | custom-call | tf_op jit(solution)/shard_map/block/pallas_call | solution.py:366
  53.3 1.6 %finish.1 = (bf16[8,1280,128]{2,1,0:T(8,128)(2,1)}, bf16[1,320,256]{2,1,0:T(8,128)(2,1)}) custom-call(bf16[8,1280,128]{2,1,0:T(8,128)(2,1)S(1)} %get-tuple-element.6.res, bf16[32,16,256]{2,1,0:T(8,128)(2,1)S(1)} %get-tuple-element.7.tok), custom_call_target="tpu_custom_call" | custom-call | tf_op jit(solution)/shard_map/finish/pallas_call | solution.py:419

commit v4 on v3

--- a/solution.py
+++ b/solution.py
@@ -18,8 +18,8 @@
 FR = 8
 ND = 32
 EDGES = (((0, 2), (2, 1), (3, 2), (5, 2), (7, 1)), ((0, 2), (2, 2), (4, 2), (6, 2)))
-SLOT_TWO = (1, 1, 1, 1, 2, 2, 3, 3)
-SLOTS = 4
+SLOT_TWO = (1, 1, 1, 1, 2, 2, 2, 2)
+SLOTS = 3
 DEPTH = 3 * C + 32
 MESH = pl.DeviceIdType.MESH
 
@@ -125,6 +125,8 @@
         (bias2_in, bias2), (w2_in, raw2), (gain2_in, gain2), (shift2_in, shift2), (order_in, order),
     ]
     others = [pltpu.make_async_copy(a, b, small_sem.at[i]) for i, (a, b) in enumerate(others)]
+    for copy in others:
+        copy.start()
 
     def halo_copies(stage, n):
         buf = (x6, h6)[stage]
@@ -235,18 +237,16 @@
             channel_stats(f, xs)
         return carry
 
+    same[...] = where_one(group_of((C, C), 0) == group_of((C, C), 1))
+    lane = lax.broadcasted_iota(jnp.int32, (C, W), 1)
+    lanes_a[...] = where_one(group_of((C, W), 0) == lane)
+    lanes_b[...] = where_one(group_of((C, W), 0) + GROUPS == lane)
     means[...] = jnp.zeros((8, C), F32)
     sqs[...] = jnp.zeros((8, C), F32)
     lax.fori_loop(0, 1, split, 0)
     pl.semaphore_wait(barrier, ND - 1)
     halo_start(0, 0)
     lax.fori_loop(1, FR // 2, split, 0)
-    for copy in others:
-        copy.start()
-    same[...] = where_one(group_of((C, C), 0) == group_of((C, C), 1))
-    lane = lax.broadcasted_iota(jnp.int32, (C, W), 1)
-    lanes_a[...] = where_one(group_of((C, W), 0) == lane)
-    lanes_b[...] = where_one(group_of((C, W), 0) + GROUPS == lane)
     stats(0)
     gather_start(0)
     for n in range(1, len(EDGES[0])):
@@ -268,7 +268,7 @@
     activate(x6, act0, 0, 0)
     for f in range(FR):
         if f in (2, 4, 6):
-            if f > 2:
+            if SLOT_TWO[f - 1] != SLOT_TWO[f]:
                 stats(SLOT_TWO[f - 1])
                 gather_start(SLOT_TWO[f - 1])
             halo_wait(0, f // 2 + 1)
@@ -328,15 +328,18 @@
         tok_copy(k).wait()
         return carry
 
+    trecv[me] = tsend[me]
     for k in range(1, ND):
         tok_copy(k).start()
-    trecv[me] = tsend[me]
-
-    for f in range(FR):
-        buf = (wide, wide2)[f % 2]
-        for r in range(R):
-            buf[pl.ds(r, C, stride=R), :] = resbuf[f, r].astype(F32)
-        res[f] = buf[...].astype(BF16)
+
+    def weave(i, carry):
+        for p, buf in enumerate((wide, wide2)):
+            for r in range(R):
+                buf[pl.ds(r, C, stride=R), :] = resbuf[i * 2 + p, r].astype(F32)
+            res[i * 2 + p] = buf[...].astype(BF16)
+        return carry
+
+    lax.fori_loop(0, FR // 2, weave, 0)
 
     lax.fori_loop(1, ND, tok_wait, 0)
     tok[...] = trecv[...]

time: 55.3 us -> 53.7 us (0.971)
  Pallas kernels: 54.3 us -> 52.7 us
    pallas_call x1, Pallas kernels: 52.7 us -> 51.1 us  [body(): pl.pallas_call(main_kernel, out_shape=(pltpu.VMEM((FR, C * R, W), BF16),...]
where the time goes in v4:
time: 53.7 us; the launch traced here: 53.6 us
  Pallas kernels  52.7 us (98%)
  between operations  0.82 us (2%)
    pallas_call x1, Pallas kernels, body(): pl.pallas_call(main_kernel, out_shape=(pltpu.VMEM((FR, C * R, W), BF16),...  51.1 us
    pallas_call x1, Pallas kernels, body(): pl.pallas_call(finish_kernel, out_shape=(jax.ShapeDtypeStruct((FR, C * R,...  1.61 us

profile of v4, /device:TPU:1, one launch (start us, length us, event | category | flops | bytes accessed | tf_op | source)
XLA Modules:
  0.0 53.6 jit_solution(16741685630622618181)
XLA Ops:
  0.6 51.1 %block.1 = (bf16[8,1280,128]{2,1,0:T(8,128)(2,1)S(1)}, bf16[32,16,256]{2,1,0:T(8,128)(2,1)S(1)}) custom-call(bf16[8,1280,128]{2,1,0:T(8,128)(2,1)} %bitcast.5, bf16[8,1280]{1,0:T(8,128)(2,1)} %temb_in.1, bf16[320,1280]{1,0:T(8,128)(2,1)} %bitcast.8, f32[320]{0:T(512)} %gain1_in.1, f32[320]{0:T(512)} %shift1_in.1, bf16[9,320,320]{2,1,0:T(8,128)(2,1)} %bitcast.6, ...), custom_call_target="tpu_custom_call" | custom-call | tf_op jit(solution)/shard_map/block/pallas_call | solution.py:369
  51.8 1.6 %finish.1 = (bf16[8,1280,128]{2,1,0:T(8,128)(2,1)}, bf16[1,320,256]{2,1,0:T(8,128)(2,1)}) custom-call(bf16[8,1280,128]{2,1,0:T(8,128)(2,1)S(1)} %get-tuple-element.6.res, bf16[32,16,256]{2,1,0:T(8,128)(2,1)S(1)} %get-tuple-element.7.tok), custom_call_target="tpu_custom_call" | custom-call | tf_op jit(solution)/shard_map/finish/pallas_call | solution.py:422
